TPU v7x, 32 devices: a whole 2x2x4 slice. The times are simulated.
32 devices in a mesh: groups: 2 (over x), expert: 4 (over y, core), dp: 4 (over z).
Axes of the slice: x: 2, y: 2, z: 4, core: 2. Of those that a mesh axis runs over, the one named last changes fastest.
Arguments:
- tokens: bfloat16 [4096, 2048], P(('groups', 'expert', 'dp')), parts along dimension 0, may hold values from -6 to 6
- out_grad: bfloat16 [4096, 2048], P(('groups', 'expert', 'dp')), parts along dimension 0, may hold values from -6 to 6
- routes: int32 [4096, 2], P(('groups', 'expert', 'dp')), parts along dimension 0, may hold values from 0 to 3, all different within a row; in each aligned block of 128 rows (0 to 127, 128 to 255, ...) at most 128 rows name the same one
- route_gates: bfloat16 [4096, 2], P(('groups', 'expert', 'dp')), parts along dimension 0, may hold values from 0.049804688 to 1
- w_gate: bfloat16 [4, 2048, 768], P('expert'), may hold values from -0.125 to 0.125
- w_up: bfloat16 [4, 2048, 768], P('expert'), may hold values from -0.125 to 0.125
- w_down: bfloat16 [4, 768, 2048], P('expert'), may hold values from -0.21875 to 0.21875
Outputs:
- grad_tokens: bfloat16 [4096, 2048], P(('groups', 'expert', 'dp')), parts along dimension 0
- grad_gates: bfloat16 [4096, 2], P(('groups', 'expert', 'dp')), parts along dimension 0
- grad_gate: bfloat16 [8, 2048, 768], P(('groups', 'expert'), 'dp'), parts along dimension 0
- grad_up: bfloat16 [8, 2048, 768], P(('groups', 'expert'), 'dp'), parts along dimension 0
- grad_down: bfloat16 [8, 768, 2048], P(('groups', 'expert'), None, 'dp'), parts along dimension 0
There are 2 independent parts, one for each index of `groups`. A program takes and returns all parts, laid end to end along the dimension named above; an argument that names none is the same for every part. Nothing has to cross between parts.
Inputs may be any that keep to these rules, and one draw needn't show every extreme that they name: `routes`: each token names 2 different experts. Within the 128 rows of one device no expert is named more than 128 times, and in every draw some expert is named exactly 128 times by the rows of some device.
All inputs are finite; a program needn't handle non-finite values.
Results may differ from a plain program's by a relative error of at most 0.0059.
Values may be sent and summed in bfloat16 or wider, within the bound.
A program may use at most 128 MiB of HBM per device.

v0:
```python
import jax
import jax.numpy as jnp
from jax import lax
from jax.sharding import PartitionSpec as P


def expert_rows(token_rows, grad_rows, gate_rows, gate_mat, up_mat, down_mat):
    pre_gate = jnp.dot(token_rows, gate_mat, preferred_element_type=jnp.float32)
    pre_up = jnp.dot(token_rows, up_mat, preferred_element_type=jnp.float32)
    sigmoid_gate = jax.nn.sigmoid(pre_gate)
    activated = pre_gate * sigmoid_gate
    hidden = (activated * pre_up).astype(jnp.bfloat16)
    back_proj = jnp.einsum("rd,hd->rh", grad_rows, down_mat, preferred_element_type=jnp.float32)
    expert_output = jnp.dot(hidden, down_mat, preferred_element_type=jnp.float32)
    gate_grad = jnp.sum(expert_output * grad_rows.astype(jnp.float32), axis=1)
    gate_scale = gate_rows.astype(jnp.float32)[:, None]
    scaled_back = gate_scale * back_proj
    grad_pre_gate = (
        scaled_back * pre_up * sigmoid_gate * (1.0 + pre_gate * (1.0 - sigmoid_gate))
    ).astype(jnp.bfloat16)
    grad_pre_up = (scaled_back * activated).astype(jnp.bfloat16)
    route_grad = (
        jnp.einsum("rh,dh->rd", grad_pre_gate, gate_mat, preferred_element_type=jnp.float32)
        + jnp.einsum("rh,dh->rd", grad_pre_up, up_mat, preferred_element_type=jnp.float32)
    ).astype(jnp.bfloat16)
    scaled_grad = (gate_scale * grad_rows.astype(jnp.float32)).astype(jnp.bfloat16)
    return (
        route_grad,
        gate_grad.astype(jnp.bfloat16),
        grad_pre_gate,
        grad_pre_up,
        hidden,
        scaled_grad,
    )


def body(tokens, out_grad, routes, route_gates, w_gate, w_up, w_down):
    tok_count, top_count = routes.shape
    model_width = tokens.shape[1]
    experts_total = lax.axis_size("expert")
    route_count = tok_count * top_count
    capacity = 2 * route_count // experts_total
    slot_total = experts_total * capacity
    flat_ids = routes.reshape(-1)
    one_hot = (flat_ids[:, None] == jnp.arange(experts_total, dtype=jnp.int32)[None, :]).astype(
        jnp.int32
    )
    route_rank = jnp.sum(jnp.cumsum(one_hot, axis=0) * one_hot, axis=1) - 1
    slot_index = flat_ids * capacity + route_rank
    slot_owner = (
        jnp.full((slot_total,), route_count, jnp.int32)
        .at[slot_index]
        .set(jnp.arange(route_count, dtype=jnp.int32))
    )
    filled = slot_owner < route_count
    safe_owner = jnp.minimum(slot_owner, route_count - 1)
    token_pick = safe_owner // top_count
    zero_bf = jnp.zeros((), jnp.bfloat16)
    send_tokens = jnp.where(filled[:, None], tokens[token_pick], zero_bf).reshape(
        experts_total, capacity, model_width
    )
    send_grads = jnp.where(filled[:, None], out_grad[token_pick], zero_bf).reshape(
        experts_total, capacity, model_width
    )
    send_gates = jnp.where(filled, route_gates.reshape(-1)[safe_owner], zero_bf).reshape(
        experts_total, capacity
    )
    recv_tokens, recv_grads, recv_gates = (
        lax.all_to_all(send_tokens, "expert", split_axis=0, concat_axis=0, tiled=True),
        lax.all_to_all(send_grads, "expert", split_axis=0, concat_axis=0, tiled=True),
        lax.all_to_all(send_gates, "expert", split_axis=0, concat_axis=0, tiled=True),
    )
    slot_rows = recv_tokens.shape[0] * recv_tokens.shape[1]
    token_rows = recv_tokens.reshape(slot_rows, model_width)
    grad_rows = recv_grads.reshape(slot_rows, model_width)
    gate_rows = recv_gates.reshape(slot_rows)
    gate_mat = w_gate[0]
    up_mat = w_up[0]
    down_mat = w_down[0]
    route_grad, gate_grad, grad_pre_gate, grad_pre_up, hidden, scaled_grad = expert_rows(
        token_rows, grad_rows, gate_rows, gate_mat, up_mat, down_mat
    )
    back_grad, back_gate = (
        lax.all_to_all(
            route_grad.reshape(experts_total, capacity, model_width),
            "expert",
            split_axis=0,
            concat_axis=0,
            tiled=True,
        ),
        lax.all_to_all(
            gate_grad.reshape(experts_total, capacity),
            "expert",
            split_axis=0,
            concat_axis=0,
            tiled=True,
        ),
    )
    home_grad = back_grad.reshape(slot_total, model_width)[slot_index]
    grad_tokens = jnp.sum(
        home_grad.reshape(tok_count, top_count, model_width).astype(jnp.float32), axis=1
    ).astype(jnp.bfloat16)
    grad_gates = back_gate.reshape(slot_total)[slot_index].reshape(tok_count, top_count)
    term_gate = jnp.einsum(
        "rd,rh->dh", token_rows, grad_pre_gate, preferred_element_type=jnp.float32
    )
    term_up = jnp.einsum("rd,rh->dh", token_rows, grad_pre_up, preferred_element_type=jnp.float32)
    term_down = jnp.einsum("rh,rd->hd", hidden, scaled_grad, preferred_element_type=jnp.float32)
    shares = (
        lax.psum_scatter(term_gate, "dp", scatter_dimension=0, tiled=True),
        lax.psum_scatter(term_up, "dp", scatter_dimension=0, tiled=True),
        lax.psum_scatter(term_down, "dp", scatter_dimension=1, tiled=True),
    )
    grad_gate = shares[0].astype(jnp.bfloat16)[None]
    grad_up = shares[1].astype(jnp.bfloat16)[None]
    grad_down = shares[2].astype(jnp.bfloat16)[None]
    return (grad_tokens, grad_gates, grad_gate, grad_up, grad_down)


def solution(mesh):
    placed = (
        P(("groups", "expert", "dp"), None),
        P(("groups", "expert", "dp"), None),
        P(("groups", "expert", "dp"), None),
        P(("groups", "expert", "dp"), None),
        P("expert", None, None),
        P("expert", None, None),
        P("expert", None, None),
    )
    return jax.shard_map(
        body,
        mesh=mesh,
        in_specs=placed,
        out_specs=(
            P(("groups", "expert", "dp"), None),
            P(("groups", "expert", "dp"), None),
            P(("groups", "expert"), "dp", None),
            P(("groups", "expert"), "dp", None),
            P(("groups", "expert"), None, "dp"),
        ),
        check_vma=False,
    )
```

profile of v0, /device:TPU:0, one launch (start us, length us, event | category | flops | bytes accessed | tf_op | source)
XLA Modules:
  0.0 462.0 jit_solution(14768663741775065105)
XLA Ops:
  10.4 1.2 reduce-window.6
  12.1 1.4 scatter_custom_fusion
  13.5 3.4 gather_fusion
  17.5 4.2 all-to-all-start
  21.7 6.3 %gather_fusion.2 = bf16[512,2048]{1,0:T(8,128)(2,1)} fusion(bf16[128,2048]{1,0:T(8,128)(2,1)} %param.7, s32[1024]{0:T(1024)S(1)} %get-tuple-element.24), kind=kCustom, calls=%fused_computation.2 | custom fusion | bytes 4196352 | tf_op jit(solution)/shard_map/gather | solution.py:59
  28.1 6.4 %gather_fusion.1 = bf16[512,2048]{1,0:T(8,128)(2,1)} fusion(bf16[128,2048]{1,0:T(8,128)(2,1)} %param.8, s32[1024]{0:T(1024)S(1)} %get-tuple-element.24), kind=kCustom, calls=%fused_computation.1 | custom fusion | bytes 4196352 | tf_op jit(solution)/shard_map/gather | solution.py:62
  34.4 4.5 broadcast_select_fusion.1
  38.9 30.2 %all_to_all.30 = bf16[4,128,2048]{2,1,0:T(8,128)(2,1)} all-to-all(bf16[4,128,2048]{2,1,0:T(8,128)(2,1)} %get-tuple-element.23), channel_id=1, replica_groups=mesh['groups'=2,'expert'=4,'dp'=4] {'expert'}, dimensions={0} | all-to-all | bytes 4194304 | tf_op jit(solution)/shard_map/all_to_all | solution.py:69
  69.1 4.4 all-to-all-start.1
  73.8 5.5 %fusion.4 = f32[512,768]{1,0:T(8,128)} fusion(bf16[512,2048]{1,0:T(8,128)(2,1)} %bitcast.71, bf16[1,2048,768]{2,1,0:T(8,128)(2,1)} %param.11), kind=kOutput, calls=%fused_computation.13 | convolution fusion | flops 1610612736 | bytes 6815744 | tf_op jit(solution)/shard_map/dot_general | solution.py:8
  79.3 20.1 %all-to-all-done.1 = bf16[4,128,2048]{2,1,0:T(8,128)(2,1)} async-done(((bf16[4,128,2048]{2,1,0:T(8,128)(2,1)}), bf16[4,128,2048]{2,1,0:T(8,128)(2,1)}, u32[]{:S(2)}, u32[]{:S(2)}) %all-to-all-start.1) | async-done | bytes 2097184 | tf_op jit(solution)/shard_map/all_to_all | solution.py:70
  99.3 4.5 fusion.19
  103.9 3.4 multiply_convert_fusion
  108.1 6.1 %fusion.15 = f32[768,2048]{1,0:T(8,128)} fusion(bf16[512,768]{1,0:T(8,128)(2,1)S(1)} %get-tuple-element.17, bf16[512,2048]{1,0:T(8,128)(2,1)} %bitcast.8, f32[512]{0:T(512)S(1)} %bitcast.79), kind=kOutput, calls=%fused_computation.22 | convolution fusion | flops 1613758464 | bytes 9177088 | tf_op jit(solution)/shard_map/rh,rd->hd/dot_general | solution.py:108
  114.3 6.3 %fusion.29 = f32[2048,768]{1,0:T(8,128)} fusion(bf16[512,2048]{1,0:T(8,128)(2,1)} %bitcast.72, bf16[512,768]{1,0:T(8,128)(2,1)} %get-tuple-element.19), kind=kOutput, calls=%fused_computation.62 | convolution fusion | flops 1610612736 | bytes 9175040 | tf_op jit(solution)/shard_map/rd,rh->dh/dot_general | solution.py:107
  120.7 7.0 %fusion.28 = f32[2048,768]{1,0:T(8,128)} fusion(bf16[512,2048]{1,0:T(8,128)(2,1)} %bitcast.73, bf16[512,768]{1,0:T(8,128)(2,1)} %get-tuple-element.18), kind=kOutput, calls=%fused_computation.61 | convolution fusion | flops 1610612736 | bytes 9175040 | tf_op jit(solution)/shard_map/rd,rh->dh/dot_general | solution.py:104
  127.7 4.7 %fusion = bf16[512]{0:T(512)(128)(2,1)S(1)} fusion(bf16[512,2048]{1,0:T(8,128)(2,1)} %bitcast.8, bf16[512,768]{1,0:T(8,128)(2,1)} %copy-done.3, bf16[1,768,2048]{2,1,0:T(8,128)(2,1)} %param.13), kind=kOutput, calls=%fused_computation.8 | convolution fusion | flops 1613757952 | bytes 6030336 | tf_op jit(solution)/shard_map/dot_general | solution.py:14
  133.0 3.4 all-to-all-start.4
  136.4 4.0 fusion.2
  140.5 3.2 add_convert_fusion
  143.6 4.4 all-to-all-start.3
  148.1 1.9 gather_fusion.4
  150.8 23.0 %all-to-all-done.3 = bf16[4,128,2048]{2,1,0:T(8,128)(2,1)} async-done(((bf16[4,128,2048]{2,1,0:T(8,128)(2,1)}), bf16[4,128,2048]{2,1,0:T(8,128)(2,1)}, u32[]{:S(2)}, u32[]{:S(2)}) %all-to-all-start.3) | async-done | bytes 2097184 | tf_op jit(solution)/shard_map/all_to_all | solution.py:84
  173.9 5.2 %gather_fusion.3 = bf16[256,2048]{1,0:T(8,128)(2,1)} fusion(bf16[512,2048]{1,0:T(8,128)(2,1)} %bitcast.15, s32[1024]{0:T(1024)S(1)} %pad_clamp_fusion), kind=kCustom, calls=%fused_computation.3 | custom fusion | bytes 2098176 | tf_op jit(solution)/shard_map/gather | solution.py:99
  179.1 2.5 reshape.134
  181.6 4.6 reduce_sum.31
  186.2 39.7 %reduce-scatter.8.cloned.1.call-done = f32[768,512]{1,0:T(8,128)} async-done(((f32[768,2048]{1,0:T(8,128)}), f32[768,512]{1,0:T(8,128)}) %reduce-scatter.8.cloned.1.call-update) | async-done | bytes 1572880 | tf_op jit(solution)/shard_map/reduce_scatter | solution.py:112
  225.9 2.4 convert_bitcast_fusion
  228.3 111.2 %reduce-scatter.6.cloned.1.call-done = f32[512,768]{1,0:T(8,128)} async-done(((f32[2048,768]{1,0:T(8,128)}), f32[512,768]{1,0:T(8,128)}) %reduce-scatter.6.cloned.1.call-update) | async-done | bytes 1572880 | tf_op jit(solution)/shard_map/reduce_scatter | solution.py:111
  339.5 2.4 convert_bitcast_fusion.1
  341.9 111.3 %reduce-scatter.4.cloned.1.call-done = f32[512,768]{1,0:T(8,128)} async-done(((f32[2048,768]{1,0:T(8,128)}), f32[512,768]{1,0:T(8,128)}) %reduce-scatter.4.cloned.1.call-update) | async-done | bytes 1572880 | tf_op jit(solution)/shard_map/reduce_scatter | solution.py:110
  453.1 2.4 convert_bitcast_fusion.2
  (47 shorter events, 6.9 us)
Async XLA Ops:
  7.2 96.7 %copy-start = (bf16[1,2048,768]{2,1,0:T(8,128)(2,1)S(1)}, bf16[1,2048,768]{2,1,0:T(8,128)(2,1)}, u32[]{:S(2)}) copy-start(bf16[1,2048,768]{2,1,0:T(8,128)(2,1)} %param.12) | copy-start | bytes 9437188
  17.5 21.4 %all-to-all-start = ((bf16[4,1,128]{2,1,0:T(2,128)(2,1)}), bf16[4,1,128]{2,1,0:T(2,128)(2,1)S(1)}, u32[]{:S(2)}, u32[]{:S(2)}) async-start(bf16[4,1,128]{2,1,0:T(2,128)(2,1)} %copy.27), calls=%async_computation | async-start | bytes 4096 | tf_op jit(solution)/shard_map/all_to_all | solution.py:71
  69.1 30.2 %all-to-all-start.1 = ((bf16[4,128,2048]{2,1,0:T(8,128)(2,1)}), bf16[4,128,2048]{2,1,0:T(8,128)(2,1)}, u32[]{:S(2)}, u32[]{:S(2)}) async-start(bf16[4,128,2048]{2,1,0:T(8,128)(2,1)} %get-tuple-element.22), calls=%async_computation.1 | async-start | bytes 4194304 | tf_op jit(solution)/shard_map/all_to_all | solution.py:70
  73.6 152.3 %reduce-scatter.8.cloned.1.call-start = ((), (), s32[]{:S(2)}) async-start(), calls=%async_computation.10 | async-start | bytes 7864320 | tf_op jit(solution)/shard_map/reduce_scatter | solution.py:112
  99.3 4.5 copy-start.1
  99.3 4.5 copy-start.4
  107.2 0.9 copy-start.3
  114.3 225.2 %reduce-scatter.6.cloned.1.call-start = ((), (), s32[]{:S(2)}) async-start(), calls=%async_computation.9 | async-start | bytes 7864320 | tf_op jit(solution)/shard_map/reduce_scatter | solution.py:111
  120.6 332.5 %reduce-scatter.4.cloned.1.call-start = ((), (), s32[]{:S(2)}) async-start(), calls=%async_computation.8 | async-start | bytes 7864320 | tf_op jit(solution)/shard_map/reduce_scatter | solution.py:110
  133.0 10.7 %all-to-all-start.4 = ((bf16[4,1,128]{2,1,0:T(2,128)(2,1)}), bf16[4,1,128]{2,1,0:T(2,128)(2,1)S(1)}, u32[]{:S(2)}, u32[]{:S(2)}) async-start(bf16[4,1,128]{2,1,0:T(2,128)(2,1)} %copy.28), calls=%async_computation.4 | async-start | bytes 4096 | tf_op jit(solution)/shard_map/all_to_all | solution.py:91
  136.4 4.0 copy-start.2
  143.6 30.2 %all-to-all-start.3 = ((bf16[4,128,2048]{2,1,0:T(8,128)(2,1)}), bf16[4,128,2048]{2,1,0:T(8,128)(2,1)}, u32[]{:S(2)}, u32[]{:S(2)}) async-start(bf16[4,128,2048]{2,1,0:T(8,128)(2,1)} %bitcast.77), calls=%async_computation.3 | async-start | bytes 4194304 | tf_op jit(solution)/shard_map/all_to_all | solution.py:84
Sparse Core Ops, SparseCore 0:
  114.4 111.4 reduce-scatter.7
  228.2 111.2 reduce-scatter.5
  341.8 111.2 reduce-scatter.3
where the time goes:
time: 463 us; the launch traced here: 462 us
  waiting for transfers between devices  305 us (66%)
  matrix products  44.6 us (10%)
  local copies, waits for them, and re-layouts  32.6 us (7%)
  blocking collectives  30.2 us (7%)
  other arithmetic  18.4 us (4%)
  starting transfers between devices  16.9 us (4%)
  between operations  13.9 us (3%)
    reduce_scatter x1, waiting for transfers between devices, body(): lax.psum_scatter(term_gate, 'dp', scatter_dimension=0, tiled=True)  111 us
    reduce_scatter x1, waiting for transfers between devices, body(): lax.psum_scatter(term_up, 'dp', scatter_dimension=0, tiled=True)  111 us
    reduce_scatter x1, waiting for transfers between devices, body(): lax.psum_scatter(term_down, 'dp', scatter_dimension=1, tiled=True)  39.7 us
    all_to_all x1, blocking collectives, body(): lax.all_to_all(send_tokens, 'expert', split_axis=0, concat_axis=0, tiled=...  30.2 us
    all_to_all x1, waiting for transfers between devices, body(): lax.all_to_all(route_grad.reshape(experts_total, capacity, model_width),...  23 us
    all_to_all x1, waiting for transfers between devices, body(): lax.all_to_all(send_grads, 'expert', split_axis=0, concat_axis=0, tiled=T...  20.1 us
  transfers between devices with their start and end apart: 7, of which 5 were waited for; matrix products, arithmetic and copies ran while one was open for 15% of the time, Pallas kernels for 0%

commit v1 on v0

--- a/solution.py
+++ b/solution.py
@@ -1,7 +1,297 @@
+import functools
 import jax
 import jax.numpy as jnp
 from jax import lax
+from jax.experimental import pallas as pl
+from jax.experimental.pallas import tpu as pltpu
 from jax.sharding import PartitionSpec as P
+
+MESH = pl.DeviceIdType.MESH
+F32 = jnp.float32
+BF16 = jnp.bfloat16
+LANES = 128
+PIECES = ((0, 32, "both"), (32, 48, "own"), (80, 48, "own"))
+H_TILE = 256
+D_TILE = 256
+
+
+def dot_nt(a, b):
+    return lax.dot_general(a, b, (((1,), (1,)), ((), ())), preferred_element_type=F32)
+
+
+def dot_tn(a, b):
+    return lax.dot_general(a, b, (((0,), (0,)), ((), ())), preferred_element_type=F32)
+
+
+def layer_kernel(
+    n_expert, n_dp,
+    tok_ref, og_ref, routes_ref, gates_ref, wg_hbm, wu_hbm, wd_hbm,
+    gtok_out, ggate_out, dg_out, du_out, dd_out,
+    blocks, wg, wu, wd, acc_g, acc_u, acc_d, keep_g, keep_u, gate_sum, give, got,
+    load_sem, send_sem, recv_sem, give_sem, got_sem,
+):
+    rows = tok_ref.shape[0]
+    width = tok_ref.shape[1]
+    hidden_width = wg.shape[1]
+    group_rows = n_expert * rows
+    shard = width // n_dp
+    e = lax.axis_index("expert")
+    z = lax.axis_index("dp")
+    core = e % 2
+    sibling = e + 1 - 2 * core
+    across = (e + 2) % 4
+
+    def own_rows(expert, start, count):
+        return pl.ds(pl.multiple_of(expert * rows + start, 16), count)
+
+    loads = [
+        pltpu.make_async_copy(tok_ref, blocks.at[z, own_rows(e, 0, rows), 0:width], load_sem.at[0]),
+        pltpu.make_async_copy(og_ref, blocks.at[z, own_rows(e, 0, rows), width:2 * width], load_sem.at[1]),
+        pltpu.make_async_copy(wg_hbm.at[0], wg, load_sem.at[2]),
+        pltpu.make_async_copy(wu_hbm.at[0], wu, load_sem.at[3]),
+        pltpu.make_async_copy(wd_hbm.at[0], wd, load_sem.at[4]),
+    ]
+    for load in loads:
+        load.start()
+
+    barrier = pltpu.get_barrier_semaphore()
+    for j in (1, 2, 3):
+        pl.semaphore_signal(barrier, inc=1, device_id={"expert": (e + j) % 4}, device_id_type=MESH)
+
+    @pl.when(z > 0)
+    def _():
+        pl.semaphore_signal(barrier, inc=1, device_id={"dp": z - 1}, device_id_type=MESH)
+
+    @pl.when(z < n_dp - 1)
+    def _():
+        pl.semaphore_signal(barrier, inc=1, device_id={"dp": z + 1}, device_id_type=MESH)
+
+    lane = lax.broadcasted_iota(jnp.int32, (rows, LANES), 1)
+    spread = jnp.zeros((rows, LANES), F32)
+    for k in range(2):
+        spread += jnp.where(
+            lane == routes_ref[:, k:k + 1], gates_ref[:, k:k + 1].astype(F32), 0.0
+        )
+    blocks[z, own_rows(e, 0, rows), 2 * width:2 * width + LANES] = spread.astype(BF16)
+
+    pl.semaphore_wait(barrier, 3 + jnp.minimum(z, 1) + jnp.minimum(n_dp - 1 - z, 1))
+
+    loads[0].wait()
+    loads[1].wait()
+
+    def source_of(step):
+        half = z // 2
+        near = z + half * (3 - 2 * z)
+        last = step // 3
+        inner = last * 3 + (1 - last) * ((step + 1) % 3)
+        place = (1 - near) * step + near * inner
+        return place + half * (3 - 2 * place)
+
+    def piece_copy(kind, src, expert, other, p, target):
+        start, count, _ = PIECES[p]
+        ref = blocks.at[src, own_rows(expert, start, count), :]
+        return pltpu.make_async_remote_copy(
+            src_ref=ref, dst_ref=ref,
+            send_sem=send_sem.at[kind, src, other, p],
+            recv_sem=recv_sem.at[src, expert, p],
+            device_id=target, device_id_type=MESH,
+        )
+
+    def each_send(step, src, other, p, act):
+        expert = across if other else e
+        both = PIECES[p][2] == "both"
+        if both or not other:
+            @pl.when(jnp.logical_and(src <= z, z < n_dp - 1))
+            def _():
+                act(piece_copy(0, src, expert, other, p, {"dp": z + 1}))
+
+            @pl.when(jnp.logical_and(src >= z, z > 0))
+            def _():
+                act(piece_copy(1, src, expert, other, p, {"dp": z - 1}))
+        if not other:
+            if both:
+                @pl.when(step == 0)
+                def _():
+                    act(piece_copy(2, src, expert, other, p, {"expert": across}))
+            else:
+                act(piece_copy(2, src, expert, other, p, {"expert": across}))
+        act(piece_copy(3, src, expert, other, p, {"expert": sibling}))
+
+    def move(step):
+        src = source_of(step)
+        for other in (0, 1):
+            expert = across if other else e
+            for p in range(len(PIECES)):
+                arrival = piece_copy(3, src, expert, other, p, {"expert": sibling})
+                if other:
+                    arrival.wait_recv()
+                else:
+                    @pl.when(step > 0)
+                    def _():
+                        arrival.wait_recv()
+                each_send(step, src, other, p, lambda c: c.start())
+
+    def await_sibling(step):
+        src = source_of(step)
+        for other in (0, 1):
+            expert = (sibling + 2) % 4 if other else sibling
+            for p in range(len(PIECES)):
+                piece_copy(3, src, expert, other, p, {"expert": sibling}).wait_recv()
+
+    def compute(step):
+        src = source_of(step)
+        wide = lax.broadcasted_iota(jnp.int32, (group_rows, LANES), 1)
+        gate = jnp.sum(
+            jnp.where(wide == e, blocks[src, :, 2 * width:2 * width + LANES].astype(F32), 0.0),
+            axis=1, keepdims=True,
+        )
+        mine = pl.ds(pl.multiple_of(z * shard, LANES), shard)
+        mine_og = pl.ds(pl.multiple_of(width + z * shard, LANES), shard)
+        gate_sum[...] = jnp.zeros_like(gate_sum)
+
+        def h_step(i, carry):
+            hs = pl.ds(pl.multiple_of(i * H_TILE, H_TILE), H_TILE)
+            x = blocks[src, :, 0:width]
+            pre_gate = jnp.dot(x, wg[:, hs], preferred_element_type=F32)
+            pre_up = jnp.dot(x, wu[:, hs], preferred_element_type=F32)
+            back = dot_nt(blocks[src, :, width:2 * width], wd[hs, :])
+            sig = jax.nn.sigmoid(pre_gate)
+            act = pre_gate * sig
+            hidden = (act * pre_up).astype(BF16)
+            gate_sum[...] += jnp.sum(hidden.astype(F32) * back, axis=1, keepdims=True)
+            scaled = gate * back
+            grad_g = (scaled * pre_up * sig * (1.0 + pre_gate * (1.0 - sig))).astype(BF16)
+            grad_u = (scaled * act).astype(BF16)
+            keep_g[:, hs] = grad_g
+            keep_u[:, hs] = grad_u
+            xs = blocks[src, :, mine]
+            acc_g[:, hs] += dot_tn(xs, grad_g)
+            acc_u[:, hs] += dot_tn(xs, grad_u)
+            scaled_grad = (gate * blocks[src, :, mine_og].astype(F32)).astype(BF16)
+            acc_d[hs, :] += dot_tn(hidden, scaled_grad)
+            return carry
+
+        lax.fori_loop(0, hidden_width // H_TILE, h_step, 0)
+
+    def give_copy(j):
+        return pltpu.make_async_remote_copy(
+            src_ref=give.at[(e + j) % 4], dst_ref=got.at[j - 1],
+            send_sem=give_sem.at[j - 1], recv_sem=got_sem.at[j - 1],
+            device_id={"expert": (e + j) % 4}, device_id_type=MESH,
+        )
+
+    def route_back():
+        def d_step(i, carry):
+            ds = pl.ds(pl.multiple_of(i * D_TILE, D_TILE), D_TILE)
+            total = dot_nt(keep_g[...], wg[ds, :]) + dot_nt(keep_u[...], wu[ds, :])
+            give[:, :, ds] = total.astype(BF16).reshape(n_expert, rows, D_TILE)
+            return carry
+
+        lax.fori_loop(0, width // D_TILE, d_step, 0)
+        give[:, :, width:width + LANES] = (
+            jnp.broadcast_to(gate_sum[...], (group_rows, LANES))
+            .astype(BF16).reshape(n_expert, rows, LANES)
+        )
+        for j in (1, 2, 3):
+            give_copy(j).start()
+
+    def one_step(step, carry):
+        move(step)
+
+        @pl.when(step == 0)
+        def _():
+            acc_g[...] = jnp.zeros_like(acc_g)
+            acc_u[...] = jnp.zeros_like(acc_u)
+            acc_d[...] = jnp.zeros_like(acc_d)
+            for load in loads[2:]:
+                load.wait()
+
+        await_sibling(step)
+        compute(step)
+
+        @pl.when(step == 0)
+        def _():
+            route_back()
+
+        return carry
+
+    lax.fori_loop(0, n_dp, one_step, 0)
+
+    for j in (1, 2, 3):
+        give_copy(j).wait_recv()
+    total = give[e, :, 0:width].astype(F32)
+    for j in (1, 2, 3):
+        total += got[j - 1, :, 0:width].astype(F32)
+    gtok_out[...] = total.astype(BF16)
+    picked = []
+    for k in range(2):
+        route = routes_ref[:, k:k + 1]
+        value = jnp.where(route == e, give[e, :, width:width + LANES].astype(F32), 0.0)
+        for j in (1, 2, 3):
+            value += jnp.where(
+                route == (e + 4 - j) % 4, got[j - 1, :, width:width + LANES].astype(F32), 0.0
+            )
+        picked.append(value)
+    ggate_out[...] = jnp.where(lane == 0, picked[0], picked[1])[:, 0:2].astype(BF16)
+    dg_out[0] = acc_g[...].astype(BF16)
+    du_out[0] = acc_u[...].astype(BF16)
+    dd_out[0] = acc_d[...].astype(BF16)
+
+    def drain(step, carry):
+        src = source_of(step)
+        for other in (0, 1):
+            for p in range(len(PIECES)):
+                each_send(step, src, other, p, lambda c: c.wait_send())
+        return carry
+
+    lax.fori_loop(0, n_dp, drain, 0)
+    for j in (1, 2, 3):
+        give_copy(j).wait_send()
+
+
+def gathered_body(tokens, out_grad, routes, route_gates, w_gate, w_up, w_down):
+    n_expert, n_dp = lax.axis_size("expert"), lax.axis_size("dp")
+    rows, width = tokens.shape
+    hid = w_gate.shape[2]
+    shard = width // n_dp
+    group_rows = n_expert * rows
+    vmem = pl.BlockSpec(memory_space=pltpu.VMEM)
+    hbm = pl.BlockSpec(memory_space=pl.ANY)
+    pieces = len(PIECES)
+    return pl.pallas_call(
+        functools.partial(layer_kernel, n_expert, n_dp),
+        out_shape=(
+            jax.ShapeDtypeStruct((rows, width), BF16),
+            jax.ShapeDtypeStruct((rows, 2), BF16),
+            jax.ShapeDtypeStruct((1, shard, hid), BF16),
+            jax.ShapeDtypeStruct((1, shard, hid), BF16),
+            jax.ShapeDtypeStruct((1, hid, shard), BF16),
+        ),
+        in_specs=[hbm, hbm, vmem, vmem, hbm, hbm, hbm],
+        out_specs=(vmem,) * 5,
+        scratch_shapes=[
+            pltpu.VMEM((n_dp, group_rows, 2 * width + LANES), BF16),
+            pltpu.VMEM((width, hid), BF16),
+            pltpu.VMEM((width, hid), BF16),
+            pltpu.VMEM((hid, width), BF16),
+            pltpu.VMEM((shard, hid), F32),
+            pltpu.VMEM((shard, hid), F32),
+            pltpu.VMEM((hid, shard), F32),
+            pltpu.VMEM((group_rows, hid), BF16),
+            pltpu.VMEM((group_rows, hid), BF16),
+            pltpu.VMEM((group_rows, 1), F32),
+            pltpu.VMEM((n_expert, rows, width + LANES), BF16),
+            pltpu.VMEM((n_expert - 1, rows, width + LANES), BF16),
+            pltpu.SemaphoreType.DMA((5,)),
+            pltpu.SemaphoreType.DMA((4, n_dp, 2, pieces)),
+            pltpu.SemaphoreType.DMA((n_dp, n_expert, pieces)),
+            pltpu.SemaphoreType.DMA((3,)),
+            pltpu.SemaphoreType.DMA((3,)),
+        ],
+        compiler_params=pltpu.CompilerParams(
+            collective_id=0, has_side_effects=True, vmem_limit_bytes=60 * 2**20
+        ),
+    )(tokens, out_grad, routes, route_gates, w_gate, w_up, w_down)
 
 
 def expert_rows(token_rows, grad_rows, gate_rows, gate_mat, up_mat, down_mat):
@@ -127,8 +417,9 @@
         P("expert", None, None),
         P("expert", None, None),
     )
+    small = mesh.shape["expert"] == 4 and mesh.shape["dp"] == 4
     return jax.shard_map(
-        body,
+        gathered_body if small else body,
         mesh=mesh,
         in_specs=placed,
         out_specs=(

time: 463 us -> 192 us (0.41)
  waiting for transfers between devices: 305 us -> 0 us
  Pallas kernels: 0 us -> 181 us
  matrix products: 44.6 us -> 0 us
  blocking collectives: 30.2 us -> 0 us
  local copies, waits for them, and re-layouts: 32.6 us -> 9.97 us
  other arithmetic: 18.4 us -> 0 us
  starting transfers between devices: 16.9 us -> 0 us
  between operations: 13.9 us -> 0.66 us
    reduce_scatter x3 -> x0, waiting for transfers between devices: 262 us -> none  [the longest x1 111 us: body(): lax.psum_scatter(term_gate, 'dp', scatter_dimension=0, tiled=True)]
    pallas_call x0 -> x1, Pallas kernels: none -> 181 us  [gathered_body(): pl.pallas_call(functools.partial(layer_kernel, n_expert, n_dp), out_shape...]
    dot_general x9 -> x0, matrix products: 44.6 us -> none  [the longest x1 7.04 us: body(): jnp.einsum('rd,rh->dh', token_rows, grad_pre_gate, preferred_element_type...]
    all_to_all x4 -> x0, waiting for transfers between devices: 43.1 us -> none  [the longest x1 23 us: body(): lax.all_to_all(route_grad.reshape(experts_total, capacity, model_width),...]
    all_to_all x1 -> x0, blocking collectives: 30.2 us -> none  [body(): lax.all_to_all(send_tokens, 'expert', split_axis=0, concat_axis=0, tiled=...]
    gather x5 -> x0, local copies, waits for them, and re-layouts: 23.2 us -> none  [the longest x1 6.38 us: body(): out_grad[token_pick]]
    all_to_all x4 -> x0, starting transfers between devices: 16.6 us -> none  [the longest x1 4.44 us: body(): lax.all_to_all(route_grad.reshape(experts_total, capacity, model_width),...]
    broadcast_in_dim x3 -> x0, other arithmetic: 7.11 us -> none  [the longest x1 2.39 us: body(): grad_down = shares[2].astype(jnp.bfloat16)[None]]
  transfers between devices with their start and end apart: 7 -> 0, of which waited for: 5 -> 0; matrix products, arithmetic and copies ran while one was open for 15% -> 0% of each run, Pallas kernels for 0% -> 0%
where the time goes in v1:
time: 192 us
  Pallas kernels  181 us (94%)
  local copies, waits for them, and re-layouts  9.97 us (5%)
    pallas_call x1, Pallas kernels, gathered_body(): pl.pallas_call(functools.partial(layer_kernel, n_expert, n_dp), out_shape...  181 us
    unnamed x10, local copies, waits for them, and re-layouts  8.51 us

profile of v1, /device:TPU:0, one launch (start us, length us, event | category | flops | bytes accessed | tf_op | source)
XLA Modules:
  0.0 191.6 jit_solution(14053135545909949472)
XLA Ops:
  0.6 1.4 copy.13.gates_ref
  2.0 1.4 copy.12.routes_ref
  3.4 181.0 %shard_map.110 = (bf16[128,2048]{1,0:T(8,128)(2,1)}, bf16[128,2]{1,0:T(8,128)(2,1)}, bf16[1,512,768]{2,1,0:T(8,128)(2,1)}, bf16[1,512,768]{2,1,0:T(8,128)(2,1)}, bf16[1,768,512]{2,1,0:T(8,128)(2,1)}) custom-call(bf16[128,2048]{1,0:T(8,128)(2,1)} %tok_ref.1, bf16[128,2048]{1,0:T(8,128)(2,1)} %og_ref.1, s32[128,2]{1,0:T(8,128)} %copy.12.routes_ref, ...), custom_call_target="tpu_custom_call" | custom-call | tf_op jit(solution)/shard_map/pallas_call | solution.py:261
  184.4 0.0 copy-start.1
  184.5 0.0 copy-start
  184.5 1.5 copy.14
  185.9 1.9 copy.19
  187.8 2.1 %copy.20 = bf16[1,512,768]{2,1,0:T(8,128)(2,1)} copy(bf16[1,512,768]{2,1,0:T(8,128)(2,1)} %get-tuple-element.17) | data formatting | bytes 1572864
  189.9 0.0 copy-done.1
  189.9 0.9 copy.21
  190.8 0.0 copy-done
  190.8 0.9 copy.22
Async XLA Ops:
  184.4 5.4 %copy-start.1 = (bf16[1,512,768]{2,1,0:T(8,128)(2,1)S(1)}, bf16[1,512,768]{2,1,0:T(8,128)(2,1)}, u32[]{:S(2)}) copy-start(bf16[1,512,768]{2,1,0:T(8,128)(2,1)} %get-tuple-element.18) | copy-start | bytes 2359300
  184.5 6.3 %copy-start = (bf16[1,768,512]{2,1,0:T(8,128)(2,1)S(1)}, bf16[1,768,512]{2,1,0:T(8,128)(2,1)}, u32[]{:S(2)}) copy-start(bf16[1,768,512]{2,1,0:T(8,128)(2,1)} %get-tuple-element.19) | copy-start | bytes 2359300

commit v2 on v1

--- a/solution.py
+++ b/solution.py
@@ -117,11 +117,16 @@
                 act(piece_copy(2, src, expert, other, p, {"expert": across}))
         act(piece_copy(3, src, expert, other, p, {"expert": sibling}))
 
+    def late(other, p):
+        return other == 1 and PIECES[p][2] == "own"
+
     def move(step):
         src = source_of(step)
         for other in (0, 1):
             expert = across if other else e
             for p in range(len(PIECES)):
+                if late(other, p):
+                    continue
                 arrival = piece_copy(3, src, expert, other, p, {"expert": sibling})
                 if other:
                     arrival.wait_recv()
@@ -130,6 +135,13 @@
                     def _():
                         arrival.wait_recv()
                 each_send(step, src, other, p, lambda c: c.start())
+
+    def cross(step):
+        src = source_of(step)
+        for p in range(len(PIECES)):
+            if late(1, p):
+                piece_copy(3, src, across, 1, p, {"expert": sibling}).wait_recv()
+                each_send(step, src, 1, p, lambda c: c.start())
 
     def await_sibling(step):
         src = source_of(step)
@@ -195,10 +207,12 @@
         for j in (1, 2, 3):
             give_copy(j).start()
 
-    def one_step(step, carry):
-        move(step)
-
-        @pl.when(step == 0)
+    def one_turn(turn, carry):
+        @pl.when(turn < n_dp)
+        def _():
+            move(turn)
+
+        @pl.when(turn == 0)
         def _():
             acc_g[...] = jnp.zeros_like(acc_g)
             acc_u[...] = jnp.zeros_like(acc_u)
@@ -206,16 +220,20 @@
             for load in loads[2:]:
                 load.wait()
 
-        await_sibling(step)
-        compute(step)
-
-        @pl.when(step == 0)
+        @pl.when(turn > 0)
+        def _():
+            step = turn - 1
+            cross(step)
+            await_sibling(step)
+            compute(step)
+
+        @pl.when(turn == 1)
         def _():
             route_back()
 
         return carry
 
-    lax.fori_loop(0, n_dp, one_step, 0)
+    lax.fori_loop(0, n_dp + 1, one_turn, 0)
 
     for j in (1, 2, 3):
         give_copy(j).wait_recv()

time: 192 us -> 138 us (0.72)
  Pallas kernels: 181 us -> 127 us
    pallas_call x1, Pallas kernels: 181 us -> 127 us  [gathered_body(): pl.pallas_call(functools.partial(layer_kernel, n_expert, n_dp), out_shape...]
where the time goes in v2:
time: 138 us
  Pallas kernels  127 us (92%)
  local copies, waits for them, and re-layouts  9.97 us (7%)
    pallas_call x1, Pallas kernels, gathered_body(): pl.pallas_call(functools.partial(layer_kernel, n_expert, n_dp), out_shape...  127 us
    unnamed x10, local copies, waits for them, and re-layouts  8.51 us

profile of v2, /device:TPU:0, one launch (start us, length us, event | category | flops | bytes accessed | tf_op | source)
XLA Modules:
  0.0 137.7 jit_solution(15912560622655525337)
XLA Ops:
  0.6 1.4 %copy.13.gates_ref = bf16[128,2]{1,0:T(8,128)(2,1)} copy(bf16[128,2]{0,1:T(2,128)(2,1)} %param.10) | data formatting | bytes 1024 | tf_op args[3]
  2.0 1.4 %copy.12.routes_ref = s32[128,2]{1,0:T(8,128)} copy(s32[128,2]{0,1:T(2,128)} %param.9) | data formatting | bytes 2048 | tf_op args[2]
  3.4 127.0 %shard_map.110 = (bf16[128,2048]{1,0:T(8,128)(2,1)}, bf16[128,2]{1,0:T(8,128)(2,1)}, bf16[1,512,768]{2,1,0:T(8,128)(2,1)}, bf16[1,512,768]{2,1,0:T(8,128)(2,1)}, bf16[1,768,512]{2,1,0:T(8,128)(2,1)}) custom-call(bf16[128,2048]{1,0:T(8,128)(2,1)} %tok_ref.1, bf16[128,2048]{1,0:T(8,128)(2,1)} %og_ref.1, s32[128,2]{1,0:T(8,128)} %copy.12.routes_ref, ...), custom_call_target="tpu_custom_call" | custom-call | tf_op jit(solution)/shard_map/pallas_call | solution.py:279
  130.5 0.0 copy-start.1
  130.5 0.0 copy-start
  130.5 1.5 %copy.14 = bf16[128,2]{0,1:T(2,128)(2,1)} copy(bf16[128,2]{1,0:T(8,128)(2,1)} %get-tuple-element.6) | data formatting | bytes 1024 | tf_op jit(solution)/shard_map/pallas_call | solution.py:279
  131.9 1.9 %copy.19 = bf16[128,2048]{1,0:T(8,128)(2,1)} copy(bf16[128,2048]{1,0:T(8,128)(2,1)} %get-tuple-element.15) | data formatting | bytes 1048576
  133.8 2.1 %copy.20 = bf16[1,512,768]{2,1,0:T(8,128)(2,1)} copy(bf16[1,512,768]{2,1,0:T(8,128)(2,1)} %get-tuple-element.17) | data formatting | bytes 1572864
  135.9 0.0 copy-done.1
  135.9 0.9 copy.21
  136.8 0.0 copy-done
  136.8 0.9 copy.22
Async XLA Ops:
  130.5 5.4 %copy-start.1 = (bf16[1,512,768]{2,1,0:T(8,128)(2,1)S(1)}, bf16[1,512,768]{2,1,0:T(8,128)(2,1)}, u32[]{:S(2)}) copy-start(bf16[1,512,768]{2,1,0:T(8,128)(2,1)} %get-tuple-element.18) | copy-start | bytes 2359300
  130.5 6.3 %copy-start = (bf16[1,768,512]{2,1,0:T(8,128)(2,1)S(1)}, bf16[1,768,512]{2,1,0:T(8,128)(2,1)}, u32[]{:S(2)}) copy-start(bf16[1,768,512]{2,1,0:T(8,128)(2,1)} %get-tuple-element.19) | copy-start | bytes 2359300

commit v3 on v2

--- a/solution.py
+++ b/solution.py
@@ -25,7 +25,7 @@
 
 def layer_kernel(
     n_expert, n_dp,
-    tok_ref, og_ref, routes_ref, gates_ref, wg_hbm, wu_hbm, wd_hbm,
+    tok_ref, og_ref, packed_ref, wg_hbm, wu_hbm, wd_hbm,
     gtok_out, ggate_out, dg_out, du_out, dd_out,
     blocks, wg, wu, wd, acc_g, acc_u, acc_d, keep_g, keep_u, gate_sum, give, got,
     load_sem, send_sem, recv_sem, give_sem, got_sem,
@@ -70,7 +70,7 @@
     spread = jnp.zeros((rows, LANES), F32)
     for k in range(2):
         spread += jnp.where(
-            lane == routes_ref[:, k:k + 1], gates_ref[:, k:k + 1].astype(F32), 0.0
+            lane == packed_ref[:, k:k + 1].astype(jnp.int32), packed_ref[:, 2 + k:3 + k], 0.0
         )
     blocks[z, own_rows(e, 0, rows), 2 * width:2 * width + LANES] = spread.astype(BF16)
 
@@ -207,6 +207,24 @@
         for j in (1, 2, 3):
             give_copy(j).start()
 
+    def home():
+        for j in (1, 2, 3):
+            give_copy(j).wait_recv()
+        total = give[e, :, 0:width].astype(F32)
+        for j in (1, 2, 3):
+            total += got[j - 1, :, 0:width].astype(F32)
+        gtok_out[...] = total.astype(BF16)
+        picked = []
+        for k in range(2):
+            route = packed_ref[:, k:k + 1].astype(jnp.int32)
+            value = jnp.where(route == e, give[e, :, width:width + LANES].astype(F32), 0.0)
+            for j in (1, 2, 3):
+                value += jnp.where(
+                    route == (e + 4 - j) % 4, got[j - 1, :, width:width + LANES].astype(F32), 0.0
+                )
+            picked.append(value)
+        ggate_out[...] = jnp.where(lane == 0, picked[0], picked[1])[:, 0:2].astype(BF16)
+
     def one_turn(turn, carry):
         @pl.when(turn < n_dp)
         def _():
@@ -231,26 +249,14 @@
         def _():
             route_back()
 
+        @pl.when(turn == n_dp - 1)
+        def _():
+            home()
+
         return carry
 
     lax.fori_loop(0, n_dp + 1, one_turn, 0)
 
-    for j in (1, 2, 3):
-        give_copy(j).wait_recv()
-    total = give[e, :, 0:width].astype(F32)
-    for j in (1, 2, 3):
-        total += got[j - 1, :, 0:width].astype(F32)
-    gtok_out[...] = total.astype(BF16)
-    picked = []
-    for k in range(2):
-        route = routes_ref[:, k:k + 1]
-        value = jnp.where(route == e, give[e, :, width:width + LANES].astype(F32), 0.0)
-        for j in (1, 2, 3):
-            value += jnp.where(
-                route == (e + 4 - j) % 4, got[j - 1, :, width:width + LANES].astype(F32), 0.0
-            )
-        picked.append(value)
-    ggate_out[...] = jnp.where(lane == 0, picked[0], picked[1])[:, 0:2].astype(BF16)
     dg_out[0] = acc_g[...].astype(BF16)
     du_out[0] = acc_u[...].astype(BF16)
     dd_out[0] = acc_d[...].astype(BF16)
@@ -276,6 +282,7 @@
     vmem = pl.BlockSpec(memory_space=pltpu.VMEM)
     hbm = pl.BlockSpec(memory_space=pl.ANY)
     pieces = len(PIECES)
+    packed = jnp.concatenate([routes.astype(F32), route_gates.astype(F32)], axis=1)
     return pl.pallas_call(
         functools.partial(layer_kernel, n_expert, n_dp),
         out_shape=(
@@ -285,7 +292,7 @@
             jax.ShapeDtypeStruct((1, shard, hid), BF16),
             jax.ShapeDtypeStruct((1, hid, shard), BF16),
         ),
-        in_specs=[hbm, hbm, vmem, vmem, hbm, hbm, hbm],
+        in_specs=[hbm, hbm, vmem, hbm, hbm, hbm],
         out_specs=(vmem,) * 5,
         scratch_shapes=[
             pltpu.VMEM((n_dp, group_rows, 2 * width + LANES), BF16),
@@ -309,7 +316,7 @@
         compiler_params=pltpu.CompilerParams(
             collective_id=0, has_side_effects=True, vmem_limit_bytes=60 * 2**20
         ),
-    )(tokens, out_grad, routes, route_gates, w_gate, w_up, w_down)
+    )(tokens, out_grad, packed, w_gate, w_up, w_down)
 
 
 def expert_rows(token_rows, grad_rows, gate_rows, gate_mat, up_mat, down_mat):

time: 138 us -> 136 us (0.986)
  local copies, waits for them, and re-layouts: 9.97 us -> 7.92 us
    unnamed x10 -> x8, local copies, waits for them, and re-layouts: 8.51 us -> 5.71 us
where the time goes in v3:
time: 136 us
  Pallas kernels  126 us (93%)
  local copies, waits for them, and re-layouts  7.92 us (6%)
    pallas_call x1, Pallas kernels, gathered_body(): pl.pallas_call(functools.partial(layer_kernel, n_expert, n_dp), out_shape...  126 us
    unnamed x8, local copies, waits for them, and re-layouts  5.71 us

profile of v3, /device:TPU:0, one launch (start us, length us, event | category | flops | bytes accessed | tf_op | source)
XLA Modules:
  0.0 136.2 jit_solution(15002238506335196356)
XLA Ops:
  0.6 0.7 convert_element_type.6
  1.3 0.7 convert_element_type.7
  2.0 0.7 copy.15.packed_ref
  2.7 126.3 %shard_map.110 = (bf16[128,2048]{1,0:T(8,128)(2,1)}, bf16[128,2]{1,0:T(8,128)(2,1)}, bf16[1,512,768]{2,1,0:T(8,128)(2,1)}, bf16[1,512,768]{2,1,0:T(8,128)(2,1)}, bf16[1,768,512]{2,1,0:T(8,128)(2,1)}) custom-call(bf16[128,2048]{1,0:T(8,128)(2,1)} %tok_ref.1, bf16[128,2048]{1,0:T(8,128)(2,1)} %og_ref.1, f32[128,4]{1,0:T(8,128)} %copy.15.packed_ref, ...), custom_call_target="tpu_custom_call" | custom-call | tf_op jit(solution)/shard_map/pallas_call | solution.py:286
  129.0 0.0 copy-start.1
  129.0 0.0 copy-start
  129.0 1.5 %copy.16 = bf16[128,2]{0,1:T(2,128)(2,1)} copy(bf16[128,2]{1,0:T(8,128)(2,1)} %get-tuple-element.11) | data formatting | bytes 1024 | tf_op jit(solution)/shard_map/pallas_call | solution.py:286
  130.5 1.9 %copy.21 = bf16[128,2048]{1,0:T(8,128)(2,1)} copy(bf16[128,2048]{1,0:T(8,128)(2,1)} %get-tuple-element.20) | data formatting | bytes 1048576
  132.4 2.1 %copy.22 = bf16[1,512,768]{2,1,0:T(8,128)(2,1)} copy(bf16[1,512,768]{2,1,0:T(8,128)(2,1)} %get-tuple-element.22) | data formatting | bytes 1572864
  134.4 0.0 copy-done.1
  134.4 0.9 copy.23
  135.3 0.0 copy-done
  135.3 0.9 copy.24
  (1 shorter events, 0.0 us)
Async XLA Ops:
  129.0 5.4 %copy-start.1 = (bf16[1,512,768]{2,1,0:T(8,128)(2,1)S(1)}, bf16[1,512,768]{2,1,0:T(8,128)(2,1)}, u32[]{:S(2)}) copy-start(bf16[1,512,768]{2,1,0:T(8,128)(2,1)} %get-tuple-element.23) | copy-start | bytes 2359300
  129.0 6.3 %copy-start = (bf16[1,768,512]{2,1,0:T(8,128)(2,1)S(1)}, bf16[1,768,512]{2,1,0:T(8,128)(2,1)}, u32[]{:S(2)}) copy-start(bf16[1,768,512]{2,1,0:T(8,128)(2,1)} %get-tuple-element.24) | copy-start | bytes 2359300
